TPU v7x, 256 devices: a whole 4x4x8 slice. The times are simulated.
256 devices in a mesh: dp: 16 (over z, x_hi), expert: 16 (over x_lo, y, core).
Axes of the slice: x: 4 (x_hi: 2, x_lo: 2; x = x_hi * 2 + x_lo), y: 4, z: 8, core: 2. Of those that a mesh axis runs over, the one named last changes fastest.
Arguments:
- acts: bfloat16 [16, 8192, 4096], P('expert', 'dp'), may hold values from -6 to 6
- out_grads: bfloat16 [16, 8192, 1024], P('expert', 'dp'), may hold values from -0.119628906 to 0.119628906
- master: float32 [16, 4096, 1024], P('expert', 'dp')
- moment_one: float32 [16, 4096, 1024], P('expert', 'dp'), may hold values from -6 to 6
- moment_two: float32 [16, 4096, 1024], P('expert', 'dp'), may hold values from 0.5 to 5
- routing: int32 [16, 16, 16], P('expert', 'dp'), may hold values from 0 to 15, each once within a row
- group_of: int32 [16], replicated, may hold values from 0 to 15, each once
Outputs:
- new_master: float32 [16, 4096, 1024], P('expert', 'dp')
- new_moment_one: float32 [16, 4096, 1024], P('expert', 'dp')
- new_moment_two: float32 [16, 4096, 1024], P('expert', 'dp')
- rollout_blocks: bfloat16 [16, 16, 16, 1, 128, 128], P('expert', 'dp')
- rollout_scales: bfloat16 [16, 16, 16, 1], P('expert', 'dp')
Inputs may be any that keep to these rules, and one draw needn't show every extreme that they name: `routing`: each row is a permutation of the slots 0 to 15. `group_of`: a permutation of the expert groups.
All inputs are finite; a program needn't handle non-finite values. Where the computation divides by a largest or mean magnitude, that divisor is 1e-20 or more.
Results may differ from a plain program's by a relative error of at most 0.0004.
The roundings to bfloat16 on the way count: a program that leaves them out, or rounds other values in their place, can miss the bound.
Values may be sent and summed in bfloat16 or wider, within the bound.
A program may use at most 128 MiB of HBM per device.

v0:
```python
import jax
import jax.numpy as jnp
from jax import lax
from jax.sharding import PartitionSpec as P

BLOCK = 128


beta_one = 0.9
beta_two = 0.95
learn_rate = 0.01
decay_rate = 0.1
adam_eps = 1e-08
corr_one = 1.0 - 0.9**10
corr_two = 1.0 - 0.95**10


def per_device(acts, out_grads, master, moment_one, moment_two, routing, group_of):
    inputs = acts[0]
    outgrad = out_grads[0]
    own_rows = master.shape[1]
    width = master.shape[2]
    contract = (((0,), (0,)), ((), ()))
    grad = lax.psum_scatter(
        lax.dot_general(inputs, outgrad, contract, preferred_element_type=jnp.float32),
        "dp",
        scatter_dimension=0,
        tiled=True,
    )
    first = beta_one * moment_one[0] + (1.0 - beta_one) * grad
    second = beta_two * moment_two[0] + (1.0 - beta_two) * grad * grad
    weight = master[0]
    update = first / corr_one / (jnp.sqrt(second / corr_two) + adam_eps) + decay_rate * weight
    weight = weight - learn_rate * update
    per_row = own_rows // BLOCK
    per_col = width // BLOCK
    nblocks = per_row * per_col
    tiles = (
        weight.reshape(per_row, BLOCK, per_col, BLOCK)
        .transpose(0, 2, 1, 3)
        .reshape(nblocks, BLOCK * BLOCK)
    )
    scale = (jnp.max(jnp.abs(tiles), axis=1) + 1e-06).astype(jnp.bfloat16)
    quantized = (tiles / scale.astype(jnp.float32)[:, None]).astype(jnp.bfloat16)
    slot_ids = lax.broadcasted_iota(jnp.int32, (nblocks, nblocks), 0)
    placing = (routing[0, 0][None, :] == slot_ids).astype(jnp.bfloat16)
    ordered = jnp.dot(placing, quantized, preferred_element_type=jnp.float32).astype(jnp.bfloat16)
    ordered_scale = jnp.dot(placing, scale[:, None], preferred_element_type=jnp.float32)[
        :, 0
    ].astype(jnp.bfloat16)
    targets = lax.axis_size("expert")
    per_dest = nblocks // targets
    arrived, arrived_scale = (
        lax.all_to_all(
            ordered.reshape(targets, per_dest, BLOCK * BLOCK),
            "expert",
            split_axis=0,
            concat_axis=0,
            tiled=True,
        ),
        lax.all_to_all(
            ordered_scale.reshape(targets, per_dest),
            "expert",
            split_axis=0,
            concat_axis=0,
            tiled=True,
        ),
    )
    experts = group_of.shape[0]
    group_ids = lax.broadcasted_iota(jnp.int32, (experts, experts), 1)
    picking = (group_of[:, None] == group_ids).astype(jnp.bfloat16)
    by_expert = jnp.einsum(
        "eg,gkn->ekn", picking, arrived, preferred_element_type=jnp.float32
    ).astype(jnp.bfloat16)
    by_expert_scale = jnp.einsum(
        "eg,gk->ek", picking, arrived_scale, preferred_element_type=jnp.float32
    ).astype(jnp.bfloat16)
    blocks_out = by_expert.reshape(1, 1, experts, per_dest, BLOCK, BLOCK)
    scales_out = by_expert_scale.reshape(1, 1, experts, per_dest)
    return (weight[None], first[None], second[None], blocks_out, scales_out)


def solution(mesh):
    in_specs = (
        P("expert", "dp", None),
        P("expert", "dp", None),
        P("expert", "dp", None),
        P("expert", "dp", None),
        P("expert", "dp", None),
        P("expert", "dp", None),
        P(),
    )
    out_specs = (
        P("expert", "dp", None),
        P("expert", "dp", None),
        P("expert", "dp", None),
        P("expert", "dp", None, None, None, None),
        P("expert", "dp", None, None),
    )
    return jax.shard_map(
        per_device, mesh=mesh, in_specs=in_specs, out_specs=out_specs, check_vma=False
    )
```

profile of v0, /device:TPU:1, one launch (start us, length us, event | category | flops | bytes accessed | tf_op | source)
XLA Modules:
  0.0 350.9 jit_solution(12943800347691237022)
XLA Ops:
  7.2 0.0 copy-start
  7.2 0.0 reduce-scatter.2.cloned.1.call-start
  7.2 1.2 copy-done
  8.4 10.4 %fusion.1 = f32[4096,1024]{1,0:T(8,128)} fusion(bf16[1,512,4096]{2,1,0:T(8,128)(2,1)} %param.7, bf16[1,512,1024]{2,1,0:T(8,128)(2,1)S(1)} %copy-done), kind=kOutput, calls=%fused_computation.3 | convolution fusion | flops 4294967296 | bytes 22020096 | tf_op jit(solution)/shard_map/dot_general | solution.py:25
  18.8 0.0 copy-start.2
  18.8 0.0 reduce-scatter.2.cloned.1.call-update
  18.8 0.0 copy-start.4
  18.8 288.8 %reduce-scatter.2.cloned.1.call-done = f32[256,1024]{1,0:T(8,128)} async-done(((f32[4096,1024]{1,0:T(8,128)}), f32[256,1024]{1,0:T(8,128)}) %reduce-scatter.2.cloned.1.call-update) | async-done | bytes 1048592 | tf_op jit(solution)/shard_map/reduce_scatter | solution.py:24
  307.7 0.0 copy-done.2
  307.7 4.0 %fusion.20 = (f32[1,256,1024]{2,1,0:T(8,128)}, f32[256,1024]{1,0:T(8,128)S(1)}, f32[1,256,1024]{2,1,0:T(8,128)}) fusion(f32[256,1024]{1,0:T(8,128)} %reduce-scatter.2.cloned.1.call-done, f32[1,256,1024]{2,1,0:T(8,128)S(1)} %copy-done.2, f32[1,256,1024]{2,1,0:T(8,128)} %param.10, f32[1,256,1024]{2,1,0:T(8,128)} %param.9), kind=kLoop, calls=%fused_computation.29 | loop fusion | flops 3932160 | bytes 7340032 | tf_op jit(solution)/shard_map/broadcast_in_dim | solution.py:80
  311.6 0.0 copy-start.1
  311.6 0.2 copy.20
  311.8 0.0 copy-start.3
  311.8 0.1 fusion.10
  312.0 0.1 convert_element_type.44
  312.0 0.1 reshape.73
  312.1 0.0 copy-done.4
  312.1 1.2 fusion
  313.3 0.5 broadcast.31
  313.8 2.1 reduce.2
  315.9 1.2 reshape.80
  317.0 0.0 copy-done.1
  317.0 0.1 fusion.5
  317.2 0.1 copy.17
  317.3 10.8 %all_to_all.11 = bf16[16,1,1]{2,1,0:T(2,128)(2,1)S(1)} all-to-all(bf16[16,1,1]{2,1,0:T(2,128)(2,1)S(1)} %copy.17), channel_id=1, replica_groups=mesh['dp'=16,'expert'=16] {'expert'}, dimensions={0} | all-to-all | bytes 64 | tf_op jit(solution)/shard_map/all_to_all | solution.py:61
  328.1 4.0 %all-to-all-start = ((bf16[16,2,8192]{2,1,0:T(2,128)(2,1)}), bf16[16,2,8192]{2,1,0:T(2,128)(2,1)S(1)}, u32[]{:S(2)}, u32[]{:S(2)}) async-start(bf16[16,2,8192]{2,1,0:T(2,128)(2,1)} %reshape.80), calls=%async_computation.1 | async-start | bytes 1048576 | tf_op jit(solution)/shard_map/all_to_all | solution.py:54
  332.1 0.2 reduce.1
  332.3 0.0 copy-done.3
  332.3 0.7 fusion.7
  333.0 9.0 %all-to-all-done = bf16[16,2,8192]{2,1,0:T(2,128)(2,1)S(1)} async-done(((bf16[16,2,8192]{2,1,0:T(2,128)(2,1)}), bf16[16,2,8192]{2,1,0:T(2,128)(2,1)S(1)}, u32[]{:S(2)}, u32[]{:S(2)}) %all-to-all-start) | async-done | bytes 524320 | tf_op jit(solution)/shard_map/all_to_all | solution.py:54
  342.0 0.5 reshape.81
  342.5 0.7 fusion.3
  343.2 0.9 copy.21
  (2 shorter events, 0.0 us)
Async XLA Ops:
  7.2 1.2 copy-start
  7.2 300.5 %reduce-scatter.2.cloned.1.call-start = ((), (), s32[]{:S(2)}) async-start(), calls=%async_computation.3 | async-start | bytes 17825792 | tf_op jit(solution)/shard_map/reduce_scatter | solution.py:24
  18.8 288.9 %copy-start.2 = (f32[1,256,1024]{2,1,0:T(8,128)S(1)}, f32[1,256,1024]{2,1,0:T(8,128)}, u32[]{:S(2)}) copy-start(f32[1,256,1024]{2,1,0:T(8,128)} %param.11) | copy-start | bytes 3145732
  18.8 293.3 %copy-start.4 = (s32[1,1,16]{2,1,0:T(1,128)S(1)}, s32[1,1,16]{2,1,0:T(1,128)}, u32[]{:S(2)}) copy-start(s32[1,1,16]{2,1,0:T(1,128)} %param.12) | copy-start | bytes 196
  311.6 5.4 %copy-start.1 = (f32[256,1024]{1,0:T(8,128)}, f32[256,1024]{1,0:T(8,128)S(1)}, u32[]{:S(2)}) copy-start(f32[256,1024]{1,0:T(8,128)S(1)} %get-tuple-element.21) | copy-start | bytes 3145732
  311.8 20.5 %copy-start.3 = (s32[16]{0:T(128)S(1)}, s32[16]{0:T(128)}, u32[]{:S(2)}) copy-start(s32[16]{0:T(128)} %param.13) | copy-start | bytes 196
  328.1 13.9 %all-to-all-start = ((bf16[16,2,8192]{2,1,0:T(2,128)(2,1)}), bf16[16,2,8192]{2,1,0:T(2,128)(2,1)S(1)}, u32[]{:S(2)}, u32[]{:S(2)}) async-start(bf16[16,2,8192]{2,1,0:T(2,128)(2,1)} %reshape.80), calls=%async_computation.1 | async-start | bytes 1048576 | tf_op jit(solution)/shard_map/all_to_all | solution.py:54
Sparse Core Ops, SparseCore 0:
  18.9 288.6 reduce-scatter.1
where the time goes:
time: 351 us
  waiting for transfers between devices  298 us (85%)
  between operations  14.1 us (4%)
  matrix products  13 us (4%)
  blocking collectives  10.8 us (3%)
  other arithmetic  6.36 us (2%)
  local copies, waits for them, and re-layouts  4.77 us (1%)
  starting transfers between devices  4.07 us (1%)
    reduce_scatter x1, waiting for transfers between devices, per_device(): lax.psum_scatter(lax.dot_general(inputs, outgrad, contract, preferred_ele...  289 us
    all_to_all x1, blocking collectives, per_device(): lax.all_to_all(ordered_scale.reshape(targets, per_dest), 'expert', split_...  10.8 us
    dot_general x1, matrix products, per_device(): lax.dot_general(inputs, outgrad, contract, preferred_element_type=jnp.flo...  10.4 us
    all_to_all x1, waiting for transfers between devices, per_device(): lax.all_to_all(ordered.reshape(targets, per_dest, BLOCK * BLOCK), 'expert...  8.97 us
  transfers between devices with their start and end apart: 2, of which 2 were waited for; matrix products, arithmetic and copies ran while one was open for 0% of the time, Pallas kernels for 0%

commit v1 on v0

v1 whole, which is shorter than its diff:
```python
import math

import jax
import jax.numpy as jnp
from jax import lax
from jax.experimental import pallas as pl
from jax.experimental.pallas import tpu as pltpu
from jax.sharding import PartitionSpec as P

MESH = pl.DeviceIdType.MESH
BLOCK = 128
NZ = 8
ND = 16
NE = 16
OWN = 256
UC = 256
MSG = 2 * OWN + 16
LEVELS = 32766.0
FINE = 8.0
LN2 = math.log(2.0)

beta_one = 0.9
beta_two = 0.95
learn_rate = 0.01
decay_rate = 0.1
adam_eps = 1e-08
corr_one = 1.0 - 0.9**10
corr_two = 1.0 - 0.95**10


def encode(ref, halves):
    steps = []
    for h, v in enumerate(halves):
        top = jnp.max(jnp.abs(v), axis=0, keepdims=True)
        step = jnp.ceil(jnp.log(jnp.maximum(top, 2.0**-100)) * (FINE / LN2))
        inv = jnp.exp(step * (-LN2 / FINE)) * LEVELS
        ref[h * OWN : (h + 1) * OWN, :] = jnp.round(v * inv).astype(jnp.int32).astype(jnp.int16)
        steps.append(jnp.broadcast_to(step, (8, BLOCK)))
    ref[2 * OWN :, :] = jnp.concatenate(steps, axis=0).astype(jnp.int32).astype(jnp.int16)


def decode(ref):
    steps = ref[2 * OWN :, :].astype(jnp.int32).astype(jnp.float32)
    scales = jnp.exp(steps * (LN2 / FINE)) * (1.0 / LEVELS)
    return [
        ref[h * OWN : (h + 1) * OWN, :].astype(jnp.int32).astype(jnp.float32)
        * scales[8 * h : 8 * h + 1, :]
        for h in range(2)
    ]


def kernel(
    acts, grads, master, moment_one, moment_two, routing, group_of,
    master_out, one_out, two_out, blocks_out, scales_out,
    a_v, g_v, w_v, m_v, v_v, wt_v, mo_v, vo_v,
    s1_send, s1_recv, s2_send, s2_recv, x2_send, x2_recv, x1_send, x1_recv, ask, asked, reply, replied,
    stat_v, sel_v, place_v, answer_v, scale_v, r_send, r_recv,
    a_sem, in_sem, out_sem,
    s1_ss, s1_rs, s2_ss, s2_rs, x2_ss, x2_rs, x1_ss, x1_rs, ask_ss, ask_rs, rep_ss, rep_rs, r_ss, r_rs,
):
    dp = lax.axis_index("dp")
    ex = lax.axis_index("expert")
    z, xh = dp // 2, dp % 2

    def zdev(way):
        return (lax.rem(z + 1 + 6 * way, NZ) * 2 + xh, ex)

    partner = (z * 2 + 1 - xh, ex)
    mine = z * 2 + xh

    def load_acts(off, half):
        i = lax.rem(z + off, NZ) * 2 + half
        return pltpu.make_async_copy(
            acts.at[0, :, pl.ds(pl.multiple_of(i * OWN, OWN), OWN)], a_v.at[i], a_sem.at[i]
        )

    grads_copy = pltpu.make_async_copy(grads.at[0], g_v, in_sem.at[0])
    load_acts(4, 0).start()
    grads_copy.start()
    load_acts(4, 1).start()
    order = (3, 5, 2, 6, 1, 7, 0)
    for off in order:
        for half in range(2):
            load_acts(off, half).start()
    state = [
        pltpu.make_async_copy(src.at[0], dst, in_sem.at[1 + i])
        for i, (src, dst) in enumerate(((master, w_v), (moment_one, m_v), (moment_two, v_v)))
    ]
    for c in state:
        c.start()

    barrier = pltpu.get_barrier_semaphore()

    @pl.loop(1, NE)
    def _(k):
        pl.semaphore_signal(barrier, inc=1, device_id=(lax.rem(dp + k, ND), ex), device_id_type=MESH)
        pl.semaphore_signal(barrier, inc=1, device_id=(dp, lax.rem(ex + k, NE)), device_id_type=MESH)

    pl.semaphore_wait(barrier, ND - 1 + NE - 1)

    def partial(i, c):
        p = lax.dot_general(
            a_v[i],
            g_v[:, pl.ds(pl.multiple_of(c * UC, UC), UC)],
            (((0,), (0,)), ((), ())),
            preferred_element_type=jnp.float32,
        )
        return [p[:, :BLOCK], p[:, BLOCK:]]

    def add(a, b):
        return [u + v for u, v in zip(a, b)]

    def s1_copy(way, s, u):
        return pltpu.make_async_remote_copy(
            src_ref=s1_send.at[way, s, u], dst_ref=s1_recv.at[way, s, u],
            send_sem=s1_ss.at[way, s, u], recv_sem=s1_rs.at[way, s, u],
            device_id=zdev(way), device_id_type=MESH,
        )

    def s2_copy(way, s, c):
        return pltpu.make_async_remote_copy(
            src_ref=s2_send.at[way, s, c], dst_ref=s2_recv.at[way, s, c],
            send_sem=s2_ss.at[way, s, c], recv_sem=s2_rs.at[way, s, c],
            device_id=zdev(way), device_id_type=MESH,
        )

    def x2_copy(j):
        return pltpu.make_async_remote_copy(
            src_ref=x2_send.at[j], dst_ref=x2_recv.at[j],
            send_sem=x2_ss.at[j], recv_sem=x2_rs.at[j],
            device_id=partner, device_id_type=MESH,
        )

    def x1_copy(c):
        return pltpu.make_async_remote_copy(
            src_ref=x1_send.at[c], dst_ref=x1_recv.at[c],
            send_sem=x1_ss.at[c], recv_sem=x1_rs.at[c],
            device_id=partner, device_id_type=MESH,
        )

    def target(way, s):
        return lax.rem(z + 4 + (1 - 2 * way) * (-s) + NZ, NZ)

    def s1_task(way, s, u, arrived):
        v = partial(target(way, s) * 2 + u // 2, u % 2)
        if arrived:
            s1_copy(way, s - 1, u).wait_recv()
            v = add(v, decode(s1_recv.at[way, s - 1, u]))
        encode(s1_send.at[way, s, u], v)
        s1_copy(way, s, u).start()

    def x2_task(j):
        o = j // 2
        off = lax.select(o % 2 == 1, 4 - (o + 1) // 2, 4 + o // 2)
        encode(x2_send.at[j], partial(lax.rem(z + off, NZ) * 2 + 1 - xh, 2 + j % 2))
        x2_copy(j).start()

    def s2_task(way, s, c, arrived):
        v = partial(target(way, s) * 2 + xh, 2 + c)
        j = c if s == 0 else (2 * s - 1 + way) * 2 + c
        x2_copy(j).wait_recv()
        v = add(v, decode(x2_recv.at[j]))
        if arrived:
            s2_copy(way, s - 1, c).wait_recv()
            v = add(v, decode(s2_recv.at[way, s - 1, c]))
        encode(s2_send.at[way, s, c], v)
        s2_copy(way, s, c).start()

    load_acts(4, 0).wait()
    grads_copy.wait()
    load_acts(4, 1).wait()

    @pl.loop(0, 2)
    def _(k):
        s1_task(0, 0, k, False)
        s1_task(1, 0, 2 + k, False)
        x2_task(k)

    for off in order:
        for half in range(2):
            load_acts(off, half).wait()

    @pl.loop(2, 6)
    def _(j):
        x2_task(j)

    @pl.loop(0, 4)
    def _(k):
        way = k % 2
        s1_task(way, 1, 2 * (1 - way) + k // 2, False)
        s1_task(way, 1, 2 * way + k // 2, True)
        x2_task(6 + k)

    @pl.loop(0, 2)
    def _(way):
        s2_task(way, 0, way, False)

    @pl.loop(0, 4)
    def _(k):
        s1_task(0, 2, k, True)
        s1_task(1, 2, k, True)
        x2_task(10 + k)

    @pl.loop(0, 2)
    def _(way):
        s2_task(way, 1, 1 - way, False)
        s2_task(way, 1, way, True)

    @pl.loop(0, 4)
    def _(k):
        s2_task(k % 2, 2, k // 2, True)
        s1_task(0, 3, k, True)
        s1_task(1, 3, k, True)

    @pl.loop(0, 2)
    def _(c):
        x2_task(14 + c)

    @pl.loop(0, 4)
    def _(k):
        s2_task(k % 2, 3, k // 2, True)

    def s1_sum(half, c):
        u = 2 * half + c
        v = partial(z * 2 + half, c)
        for way in range(2):
            s1_copy(way, 3, u).wait_recv()
            v = add(v, decode(s1_recv.at[way, 3, u]))
        return v

    @pl.loop(0, 2)
    def _(c):
        encode(x1_send.at[c], s1_sum(1 - xh, c))
        x1_copy(c).start()

    for c in state:
        c.wait()

    def results(c):
        copies = []
        cols = pl.ds(pl.multiple_of(c * UC, UC), UC)
        for n, (src, dst) in enumerate(((mo_v, one_out), (vo_v, two_out))):
            copies.append(
                pltpu.make_async_copy(src.at[:, cols], dst.at[0, :, cols], out_sem.at[c, n])
            )
        for r in range(2):
            for h in range(2):
                b = r * 8 + 2 * c + h
                lanes = pl.ds(pl.multiple_of(c * UC + h * BLOCK, BLOCK), BLOCK)
                copies.append(
                    pltpu.make_async_copy(
                        wt_v.at[b],
                        master_out.at[0, pl.ds(r * BLOCK, BLOCK), lanes],
                        out_sem.at[c, 2 + 2 * r + h],
                    )
                )
        return copies

    def adam(weight, one, two, grad):
        first = beta_one * one + (1.0 - beta_one) * grad
        second = beta_two * two + (1.0 - beta_two) * grad * grad
        update = (first * (1.0 / corr_one)) / (
            jnp.sqrt(second * (1.0 / corr_two)) + adam_eps
        ) + decay_rate * weight
        return weight - learn_rate * update, first, second

    row_ids = lax.broadcasted_iota(jnp.int32, (BLOCK, BLOCK), 0)

    def finish(c, halves):
        for h, grad in enumerate(halves):
            cols = pl.ds(pl.multiple_of(c * UC + h * BLOCK, BLOCK), BLOCK)
            weight, first, second = adam(w_v[:, cols], m_v[:, cols], v_v[:, cols], grad)
            mo_v[:, cols] = first
            vo_v[:, cols] = second
            for r in range(2):
                b = r * 8 + 2 * c + h
                rows = slice(r * BLOCK, (r + 1) * BLOCK)
                tile = weight[rows, :]
                wt_v[b] = tile
                size = jnp.abs(tile)
                top = jnp.max(size, axis=0, keepdims=True)
                at = jnp.min(jnp.where(size == top, row_ids, BLOCK), axis=0, keepdims=True)
                one_row = row_ids == at
                stat_v[0, pl.ds(b, 1), :] = top
                stat_v[1, pl.ds(b, 1), :] = at.astype(jnp.float32)
                for n, src in enumerate((w_v, m_v, v_v)):
                    stat_v[2 + n, pl.ds(b, 1), :] = jnp.sum(
                        jnp.where(one_row, src[rows, cols], 0.0), axis=0, keepdims=True
                    )
        for copy in results(c):
            copy.start()

    @pl.loop(0, 2)
    def _(c):
        v = s1_sum(xh, c)
        x1_copy(c).wait_recv()
        finish(c, add(v, decode(x1_recv.at[c])))

    @pl.loop(0, 2)
    def _(c):
        v = partial(mine, 2 + c)
        x2_copy(14 + c).wait_recv()
        v = add(v, decode(x2_recv.at[14 + c]))
        for way in range(2):
            s2_copy(way, 3, c).wait_recv()
            v = add(v, decode(s2_recv.at[way, 3, c]))
        finish(2 + c, v)

    def ask_copy(peer, source):
        return pltpu.make_async_remote_copy(
            src_ref=ask, dst_ref=asked.at[source],
            send_sem=ask_ss.at[peer], recv_sem=ask_rs.at[source],
            device_id=(peer, ex), device_id_type=MESH,
        )

    def reply_copy(peer, source):
        return pltpu.make_async_remote_copy(
            src_ref=reply.at[peer // 8], dst_ref=replied.at[source],
            send_sem=rep_ss.at[peer], recv_sem=rep_rs.at[source],
            device_id=(peer, ex), device_id_type=MESH,
        )

    lanes = lax.broadcasted_iota(jnp.int32, (NE, BLOCK), 1)
    blocks = lax.broadcasted_iota(jnp.int32, (NE, BLOCK), 0)
    slots = lanes == lax.rem(dp, 8) * NE + blocks
    top = stat_v[0]
    most = jnp.max(top, axis=1, keepdims=True)
    lane = jnp.min(jnp.where(top == most, lanes, BLOCK), axis=1, keepdims=True)
    here = lanes == lane

    def along(x):
        return jnp.sum(jnp.where(slots, x, 0.0), axis=0, keepdims=True)

    picked = [jnp.sum(jnp.where(here, stat_v[n], 0.0), axis=1, keepdims=True) for n in range(1, 5)]
    col_at = along((blocks % 8 * BLOCK + lane).astype(jnp.float32))
    row_at = along((blocks // 8 * BLOCK).astype(jnp.float32) + picked[0])
    ask[...] = jnp.concatenate(
        [jnp.broadcast_to(row_at, (8, BLOCK)), jnp.broadcast_to(col_at, (8, BLOCK))], axis=0
    )

    @pl.loop(1, ND)
    def _(k):
        ask_copy(lax.rem(dp + k, ND), dp).start()

    asked[dp] = ask[...]
    old = [along(x) for x in picked[1:]]

    @pl.loop(1, ND)
    def _(k):
        source = lax.rem(dp + k, ND)
        ask_copy(source, source).wait_recv()

    for half in range(2):
        total = asked[8 * half]
        for n in range(1, 8):
            total = total + asked[8 * half + n]
        rows = total[0:1, :].astype(jnp.int32)
        cols = total[8:9, :].astype(jnp.int32)
        place_v[half] = (
            lax.broadcasted_iota(jnp.int32, (OWN, BLOCK), 0) == rows
        ).astype(jnp.float32).astype(jnp.bfloat16)
        sel_v[half] = jnp.dot(
            g_v[...],
            (lax.broadcasted_iota(jnp.int32, (g_v.shape[1], BLOCK), 0) == cols)
            .astype(jnp.float32)
            .astype(jnp.bfloat16),
            preferred_element_type=jnp.float32,
        )
    answer_v[...] = jnp.zeros_like(answer_v)
    groups = lax.broadcasted_iota(jnp.int32, (8, BLOCK), 1) // NE

    @pl.loop(0, ND)
    def _(o):
        half = o // 8
        chosen = jnp.dot(a_v[o], place_v[half], preferred_element_type=jnp.float32)
        dots = jnp.sum(chosen * sel_v[half], axis=0, keepdims=True)
        answer_v[half] = jnp.where(groups == lax.rem(o, 8), dots, answer_v[half])

    reply[...] = answer_v[...]

    @pl.loop(1, ND)
    def _(k):
        reply_copy(lax.rem(dp + k, ND), dp).start()

    replied[dp] = answer_v[dp // 8]

    @pl.loop(1, ND)
    def _(k):
        source = lax.rem(dp + k, ND)
        reply_copy(source, source).wait_recv()

    exact = replied[0]
    for n in range(1, ND):
        exact = exact + replied[n]
    largest = jnp.abs(adam(*old, exact[0:1, :])[0])
    scale = (largest + 1e-06).astype(jnp.bfloat16).astype(jnp.float32)
    scale = jnp.sum(jnp.where(slots, scale, 0.0), axis=1, keepdims=True)
    for b in range(NE):
        scale_v[b] = jnp.broadcast_to(scale[b : b + 1, :], (8, BLOCK))

    def roll_copy(slot, source):
        return pltpu.make_async_remote_copy(
            src_ref=r_send.at[slot], dst_ref=r_recv.at[source],
            send_sem=r_ss.at[slot], recv_sem=r_rs.at[source],
            device_id=(dp, slot), device_id_type=MESH,
        )

    def held(slot):
        b = jnp.int32(0)
        for n in range(NE):
            b = lax.select(routing[0, 0, n] == slot, jnp.int32(n), b)
        return b

    def pack(ref, b):
        wide = scale_v[b]
        ref[:BLOCK, :] = (wt_v[b] / wide[0:1, :]).astype(jnp.bfloat16)
        ref[BLOCK:, :] = jnp.broadcast_to(wide[0:1, :], (16, BLOCK)).astype(jnp.bfloat16)

    @pl.loop(1, NE)
    def _(k):
        slot = lax.rem(ex + k, NE)
        pack(r_send.at[slot], held(slot))
        roll_copy(slot, ex).start()

    pack(r_recv.at[ex], held(ex))

    @pl.loop(1, NE)
    def _(k):
        source = lax.rem(ex + k, NE)
        roll_copy(source, source).wait_recv()

    for e in range(NE):
        block = r_recv[group_of[e]]
        blocks_out[e] = block[:BLOCK, :]
        scales_out[e] = block[BLOCK:, :]

    @pl.loop(1, NE)
    def _(k):
        slot = lax.rem(ex + k, NE)
        roll_copy(slot, ex).wait_send()
        peer = lax.rem(dp + k, ND)
        ask_copy(peer, dp).wait_send()
        reply_copy(peer, dp).wait_send()

    @pl.loop(0, 2)
    def _(way):
        for n in range(2):
            s1_copy(way, 0, 2 * way + n).wait_send()
        s2_copy(way, 0, way).wait_send()
        x1_copy(way).wait_send()

        @pl.loop(1, 4)
        def _(s):
            for u in range(4):
                s1_copy(way, s, u).wait_send()
            for c in range(2):
                s2_copy(way, s, c).wait_send()

    @pl.loop(0, 2 * NZ)
    def _(j):
        x2_copy(j).wait_send()

    for c in range(4):
        for copy in results(c):
            copy.wait()


def per_device(acts, out_grads, master, moment_one, moment_two, routing, group_of):
    f32, i16, bf16 = jnp.float32, jnp.int16, jnp.bfloat16
    own, width = master.shape[1], master.shape[2]
    tokens = acts.shape[1]
    dma = pltpu.SemaphoreType.DMA
    hbm = pl.BlockSpec(memory_space=pl.ANY)
    smem = pl.BlockSpec(memory_space=pltpu.SMEM)
    vmem = pl.BlockSpec(memory_space=pltpu.VMEM)
    shape = jax.ShapeDtypeStruct
    weight, first, second, blocks, scales = pl.pallas_call(
        kernel,
        out_shape=(
            shape((1, own, width), f32),
            shape((1, own, width), f32),
            shape((1, own, width), f32),
            shape((NE, BLOCK, BLOCK), bf16),
            shape((NE, 16, BLOCK), bf16),
        ),
        in_specs=[hbm] * 5 + [smem] * 2,
        out_specs=(hbm, hbm, hbm, vmem, vmem),
        scratch_shapes=[
            pltpu.VMEM((2 * NZ, tokens, OWN), bf16),
            pltpu.VMEM((tokens, width), bf16),
            pltpu.VMEM((own, width), f32),
            pltpu.VMEM((own, width), f32),
            pltpu.VMEM((own, width), f32),
            pltpu.VMEM((NE, BLOCK, BLOCK), f32),
            pltpu.VMEM((own, width), f32),
            pltpu.VMEM((own, width), f32),
            pltpu.VMEM((2, 4, 4, MSG, BLOCK), i16),
            pltpu.VMEM((2, 4, 4, MSG, BLOCK), i16),
            pltpu.VMEM((2, 4, 2, MSG, BLOCK), i16),
            pltpu.VMEM((2, 4, 2, MSG, BLOCK), i16),
            pltpu.VMEM((2 * NZ, MSG, BLOCK), i16),
            pltpu.VMEM((2 * NZ, MSG, BLOCK), i16),
            pltpu.VMEM((2, MSG, BLOCK), i16),
            pltpu.VMEM((2, MSG, BLOCK), i16),
            pltpu.VMEM((16, BLOCK), f32),
            pltpu.VMEM((ND, 16, BLOCK), f32),
            pltpu.VMEM((2, 8, BLOCK), f32),
            pltpu.VMEM((ND, 8, BLOCK), f32),
            pltpu.VMEM((5, NE, BLOCK), f32),
            pltpu.VMEM((2, tokens, BLOCK), f32),
            pltpu.VMEM((2, own, BLOCK), bf16),
            pltpu.VMEM((2, 8, BLOCK), f32),
            pltpu.VMEM((NE, 8, BLOCK), f32),
            pltpu.VMEM((NE, BLOCK + 16, BLOCK), bf16),
            pltpu.VMEM((NE, BLOCK + 16, BLOCK), bf16),
            dma((2 * NZ,)),
            dma((4,)),
            dma((4, 6)),
            dma((2, 4, 4)),
            dma((2, 4, 4)),
            dma((2, 4, 2)),
            dma((2, 4, 2)),
            dma((2 * NZ,)),
            dma((2 * NZ,)),
            dma((2,)),
            dma((2,)),
            dma((ND,)),
            dma((ND,)),
            dma((ND,)),
            dma((ND,)),
            dma((NE,)),
            dma((NE,)),
        ],
        name="update",
        cost_estimate=pl.CostEstimate(
            flops=2 * tokens * acts.shape[2] * width, bytes_accessed=12 * 2**20, transcendentals=0
        ),
        compiler_params=pltpu.CompilerParams(
            collective_id=0, has_side_effects=True, vmem_limit_bytes=56 * 2**20
        ),
    )(acts, out_grads, master, moment_one, moment_two, routing, group_of)
    return (
        weight,
        first,
        second,
        blocks.reshape(1, 1, NE, 1, BLOCK, BLOCK),
        scales[:, 0, 0].reshape(1, 1, NE, 1),
    )


def solution(mesh):
    in_specs = (P("expert", "dp", None),) * 6 + (P(),)
    out_specs = (
        P("expert", "dp", None),
        P("expert", "dp", None),
        P("expert", "dp", None),
        P("expert", "dp", None, None, None, None),
        P("expert", "dp", None, None),
    )
    return jax.shard_map(
        per_device, mesh=mesh, in_specs=in_specs, out_specs=out_specs, check_vma=False
    )
```

time: 351 us -> 117 us (0.33)
  waiting for transfers between devices: 298 us -> 0 us
  Pallas kernels: 0 us -> 108 us
  between operations: 14.1 us -> 0.66 us
  matrix products: 13 us -> 0 us
  blocking collectives: 10.8 us -> 0 us
  other arithmetic: 6.36 us -> 0 us
  starting transfers between devices: 4.07 us -> 0 us
    reduce_scatter x1 -> x0, waiting for transfers between devices: 289 us -> none  [per_device(): lax.psum_scatter(lax.dot_general(inputs, outgrad, contract, preferred_ele...]
    pallas_call x0 -> x1, Pallas kernels: none -> 108 us  [per_device(): pl.pallas_call(kernel, out_shape=(shape((1, own, width), f32), shape((1,...]
    dot_general x5 -> x0, matrix products: 13 us -> none  [the longest x1 10.4 us: per_device(): lax.dot_general(inputs, outgrad, contract, preferred_element_type=jnp.flo...]
    all_to_all x1 -> x0, blocking collectives: 10.8 us -> none  [per_device(): lax.all_to_all(ordered_scale.reshape(targets, per_dest), 'expert', split_...]
    all_to_all x1 -> x0, waiting for transfers between devices: 8.97 us -> none  [per_device(): lax.all_to_all(ordered.reshape(targets, per_dest, BLOCK * BLOCK), 'expert...]
    all_to_all x1 -> x0, starting transfers between devices: 4.03 us -> none  [per_device(): lax.all_to_all(ordered.reshape(targets, per_dest, BLOCK * BLOCK), 'expert...]
    broadcast_in_dim x1 -> x0, other arithmetic: 3.95 us -> none  [per_device(): return (weight[None], first[None], second[None], blocks_out, scales_out)]
  transfers between devices with their start and end apart: 2 -> 0, of which waited for: 2 -> 0; matrix products, arithmetic and copies ran while one was open for 0% -> 0% of each run, Pallas kernels for 0% -> 0%
where the time goes in v1:
time: 117 us; the launch traced here: 116 us
  Pallas kernels  108 us (92%)
  local copies, waits for them, and re-layouts  7.97 us (7%)
    pallas_call x1, Pallas kernels, per_device(): pl.pallas_call(kernel, out_shape=(shape((1, own, width), f32), shape((1,...  108 us
    unnamed x8, local copies, waits for them, and re-layouts  6.38 us

profile of v1, /device:TPU:1, one launch (start us, length us, event | category | flops | bytes accessed | tf_op | source)
XLA Modules:
  0.0 116.4 jit_solution(4451108292122399050)
XLA Ops:
  0.6 107.7 %update.1 = (f32[1,256,1024]{2,1,0:T(8,128)}, f32[1,256,1024]{2,1,0:T(8,128)}, f32[1,256,1024]{2,1,0:T(8,128)}, bf16[16,128,128]{2,1,0:T(8,128)(2,1)}, bf16[16,16,128]{2,1,0:T(8,128)(2,1)}) custom-call(bf16[1,512,4096]{2,1,0:T(8,128)(2,1)} %acts.1, bf16[1,512,1024]{2,1,0:T(8,128)(2,1)} %grads.1, f32[1,256,1024]{2,1,0:T(8,128)} %master.1, ...), custom_call_target="tpu_custom_call" | custom-call | flops 4294967296 | bytes 12582912 | tf_op jit(solution)/shard_map/update/pallas_call | solution.py:477
  108.4 0.0 copy-start
  108.4 0.0 copy-start.1
  108.4 1.6 %slice_reduce_fusion = bf16[16]{0:T(256)(128)(2,1)} fusion(bf16[16,16,128]{2,1,0:T(8,128)(2,1)} %get-tuple-element.14), kind=kLoop, calls=%fused_computation | loop fusion | bytes 64 | tf_op jit(solution)/shard_map/slice | solution.py:547
  110.0 2.3 %copy.18 = f32[1,256,1024]{2,1,0:T(8,128)} copy(f32[1,256,1024]{2,1,0:T(8,128)} %get-tuple-element.30) | data formatting | bytes 2097152
  112.3 2.3 %copy.19 = f32[1,256,1024]{2,1,0:T(8,128)} copy(f32[1,256,1024]{2,1,0:T(8,128)} %get-tuple-element.31) | data formatting | bytes 2097152
  114.6 0.0 copy-done
  114.6 1.0 copy.20
  115.6 0.0 copy-done.1
  115.6 0.8 copy.21
Async XLA Ops:
  108.4 6.2 %copy-start = (f32[1,256,1024]{2,1,0:T(8,128)S(1)}, f32[1,256,1024]{2,1,0:T(8,128)}, u32[]{:S(2)}) copy-start(f32[1,256,1024]{2,1,0:T(8,128)} %get-tuple-element.32) | copy-start | bytes 3145732
  108.4 7.2 %copy-start.1 = (bf16[16,128,128]{2,1,0:T(8,128)(2,1)S(1)}, bf16[16,128,128]{2,1,0:T(8,128)(2,1)}, u32[]{:S(2)}) copy-start(bf16[16,128,128]{2,1,0:T(8,128)(2,1)} %get-tuple-element.13) | copy-start | bytes 1572868

commit v2 on v1

--- a/solution.py
+++ b/solution.py
@@ -27,6 +27,29 @@
 corr_one = 1.0 - 0.9**10
 corr_two = 1.0 - 0.95**10
 
+ORDER = (
+    0, 18, 128, 1, 19, 129, 20, 130, 141, 6, 21, 134, 7, 86,
+    68, 69, 87, 132, 133, 89, 192, 209, 74, 88, 73, 131, 138, 139,
+    75, 135, 212, 91, 72, 277, 90, 260, 78, 136, 79, 137, 77, 93,
+    197, 142, 143, 95, 92, 140, 264, 76, 280, 94, 321, 265, 281, 284,
+    268, 320, 269, 285, 384, 448, 385, 449,
+)
+HEAD = 6
+
+
+def pick(k, values):
+    if len(set(values)) == 1:
+        return jnp.int32(values[0])
+    half = len(values) // 2
+    return lax.select(k < half, pick(k, values[:half]), pick(k - half, values[half:]))
+
+
+def adam(weight, one, two, grad):
+    first = beta_one * one + (1.0 - beta_one) * grad
+    second = beta_two * two + (1.0 - beta_two) * grad * grad
+    update = first / corr_one / (jnp.sqrt(second / corr_two) + adam_eps) + decay_rate * weight
+    return weight - learn_rate * update, first, second
+
 
 def encode(ref, halves):
     steps = []
@@ -51,8 +74,8 @@
 
 def kernel(
     acts, grads, master, moment_one, moment_two, routing, group_of,
-    master_out, one_out, two_out, blocks_out, scales_out,
-    a_v, g_v, w_v, m_v, v_v, wt_v, mo_v, vo_v,
+    grad_out, blocks_out, scales_out,
+    a_v, g_v, w_v, m_v, v_v, wt_v, sum_v,
     s1_send, s1_recv, s2_send, s2_recv, x2_send, x2_recv, x1_send, x1_recv, ask, asked, reply, replied,
     stat_v, sel_v, place_v, answer_v, scale_v, r_send, r_recv,
     a_sem, in_sem, out_sem,
@@ -157,7 +180,7 @@
 
     def s2_task(way, s, c, arrived):
         v = partial(target(way, s) * 2 + xh, 2 + c)
-        j = c if s == 0 else (2 * s - 1 + way) * 2 + c
+        j = lax.select(s == 0, c, (2 * s - 1 + way) * 2 + c)
         x2_copy(j).wait_recv()
         v = add(v, decode(x2_recv.at[j]))
         if arrived:
@@ -166,60 +189,6 @@
         encode(s2_send.at[way, s, c], v)
         s2_copy(way, s, c).start()
 
-    load_acts(4, 0).wait()
-    grads_copy.wait()
-    load_acts(4, 1).wait()
-
-    @pl.loop(0, 2)
-    def _(k):
-        s1_task(0, 0, k, False)
-        s1_task(1, 0, 2 + k, False)
-        x2_task(k)
-
-    for off in order:
-        for half in range(2):
-            load_acts(off, half).wait()
-
-    @pl.loop(2, 6)
-    def _(j):
-        x2_task(j)
-
-    @pl.loop(0, 4)
-    def _(k):
-        way = k % 2
-        s1_task(way, 1, 2 * (1 - way) + k // 2, False)
-        s1_task(way, 1, 2 * way + k // 2, True)
-        x2_task(6 + k)
-
-    @pl.loop(0, 2)
-    def _(way):
-        s2_task(way, 0, way, False)
-
-    @pl.loop(0, 4)
-    def _(k):
-        s1_task(0, 2, k, True)
-        s1_task(1, 2, k, True)
-        x2_task(10 + k)
-
-    @pl.loop(0, 2)
-    def _(way):
-        s2_task(way, 1, 1 - way, False)
-        s2_task(way, 1, way, True)
-
-    @pl.loop(0, 4)
-    def _(k):
-        s2_task(k % 2, 2, k // 2, True)
-        s1_task(0, 3, k, True)
-        s1_task(1, 3, k, True)
-
-    @pl.loop(0, 2)
-    def _(c):
-        x2_task(14 + c)
-
-    @pl.loop(0, 4)
-    def _(k):
-        s2_task(k % 2, 3, k // 2, True)
-
     def s1_sum(half, c):
         u = 2 * half + c
         v = partial(z * 2 + half, c)
@@ -228,50 +197,17 @@
             v = add(v, decode(s1_recv.at[way, 3, u]))
         return v
 
-    @pl.loop(0, 2)
-    def _(c):
-        encode(x1_send.at[c], s1_sum(1 - xh, c))
-        x1_copy(c).start()
-
-    for c in state:
-        c.wait()
-
-    def results(c):
-        copies = []
+    def result(c):
         cols = pl.ds(pl.multiple_of(c * UC, UC), UC)
-        for n, (src, dst) in enumerate(((mo_v, one_out), (vo_v, two_out))):
-            copies.append(
-                pltpu.make_async_copy(src.at[:, cols], dst.at[0, :, cols], out_sem.at[c, n])
-            )
-        for r in range(2):
-            for h in range(2):
-                b = r * 8 + 2 * c + h
-                lanes = pl.ds(pl.multiple_of(c * UC + h * BLOCK, BLOCK), BLOCK)
-                copies.append(
-                    pltpu.make_async_copy(
-                        wt_v.at[b],
-                        master_out.at[0, pl.ds(r * BLOCK, BLOCK), lanes],
-                        out_sem.at[c, 2 + 2 * r + h],
-                    )
-                )
-        return copies
-
-    def adam(weight, one, two, grad):
-        first = beta_one * one + (1.0 - beta_one) * grad
-        second = beta_two * two + (1.0 - beta_two) * grad * grad
-        update = (first * (1.0 / corr_one)) / (
-            jnp.sqrt(second * (1.0 / corr_two)) + adam_eps
-        ) + decay_rate * weight
-        return weight - learn_rate * update, first, second
+        return pltpu.make_async_copy(sum_v.at[:, cols], grad_out.at[:, cols], out_sem.at[c])
 
     row_ids = lax.broadcasted_iota(jnp.int32, (BLOCK, BLOCK), 0)
 
     def finish(c, halves):
         for h, grad in enumerate(halves):
             cols = pl.ds(pl.multiple_of(c * UC + h * BLOCK, BLOCK), BLOCK)
-            weight, first, second = adam(w_v[:, cols], m_v[:, cols], v_v[:, cols], grad)
-            mo_v[:, cols] = first
-            vo_v[:, cols] = second
+            sum_v[:, cols] = grad
+            weight = adam(w_v[:, cols], m_v[:, cols], v_v[:, cols], grad)[0]
             for r in range(2):
                 b = r * 8 + 2 * c + h
                 rows = slice(r * BLOCK, (r + 1) * BLOCK)
@@ -287,17 +223,18 @@
                     stat_v[2 + n, pl.ds(b, 1), :] = jnp.sum(
                         jnp.where(one_row, src[rows, cols], 0.0), axis=0, keepdims=True
                     )
-        for copy in results(c):
-            copy.start()
-
-    @pl.loop(0, 2)
-    def _(c):
+        result(c).start()
+
+    def x1_task(c):
+        encode(x1_send.at[c], s1_sum(1 - xh, c))
+        x1_copy(c).start()
+
+    def finish_s1(c):
         v = s1_sum(xh, c)
         x1_copy(c).wait_recv()
         finish(c, add(v, decode(x1_recv.at[c])))
 
-    @pl.loop(0, 2)
-    def _(c):
+    def finish_s2(c):
         v = partial(mine, 2 + c)
         x2_copy(14 + c).wait_recv()
         v = add(v, decode(x2_recv.at[14 + c]))
@@ -305,6 +242,37 @@
             s2_copy(way, 3, c).wait_recv()
             v = add(v, decode(s2_recv.at[way, 3, c]))
         finish(2 + c, v)
+
+    load_acts(4, 0).wait()
+    grads_copy.wait()
+    load_acts(4, 1).wait()
+
+    @pl.loop(0, len(ORDER))
+    def _(k):
+        @pl.when(k == HEAD)
+        def _():
+            for off in order:
+                for half in range(2):
+                    load_acts(off, half).wait()
+            for c in state:
+                c.wait()
+
+        code = pick(k, ORDER)
+        kind = code // 64
+        way, s, u = code // 16 % 4, code // 4 % 4, code % 4
+        for n, task in enumerate(
+            (
+                lambda: s1_task(way, s, u, False),
+                lambda: s1_task(way, s, u, True),
+                lambda: x2_task(code % 64),
+                lambda: s2_task(way, s, u, False),
+                lambda: s2_task(way, s, u, True),
+                lambda: x1_task(u),
+                lambda: finish_s1(u),
+                lambda: finish_s2(u),
+            )
+        ):
+            pl.when(kind == n)(task)
 
     def ask_copy(peer, source):
         return pltpu.make_async_remote_copy(
@@ -429,10 +397,12 @@
         source = lax.rem(ex + k, NE)
         roll_copy(source, source).wait_recv()
 
+    row = jnp.zeros((16, BLOCK), jnp.float32)
     for e in range(NE):
         block = r_recv[group_of[e]]
         blocks_out[e] = block[:BLOCK, :]
-        scales_out[e] = block[BLOCK:, :]
+        row = jnp.where(lanes == e, block[BLOCK:, :].astype(jnp.float32), row)
+    scales_out[...] = row.astype(jnp.bfloat16)
 
     @pl.loop(1, NE)
     def _(k):
@@ -461,8 +431,7 @@
         x2_copy(j).wait_send()
 
     for c in range(4):
-        for copy in results(c):
-            copy.wait()
+        result(c).wait()
 
 
 def per_device(acts, out_grads, master, moment_one, moment_two, routing, group_of):
@@ -474,17 +443,15 @@
     smem = pl.BlockSpec(memory_space=pltpu.SMEM)
     vmem = pl.BlockSpec(memory_space=pltpu.VMEM)
     shape = jax.ShapeDtypeStruct
-    weight, first, second, blocks, scales = pl.pallas_call(
+    grad, blocks, scales = pl.pallas_call(
         kernel,
         out_shape=(
-            shape((1, own, width), f32),
-            shape((1, own, width), f32),
-            shape((1, own, width), f32),
+            shape((own, width), f32),
             shape((NE, BLOCK, BLOCK), bf16),
-            shape((NE, 16, BLOCK), bf16),
+            shape((16, BLOCK), bf16),
         ),
         in_specs=[hbm] * 5 + [smem] * 2,
-        out_specs=(hbm, hbm, hbm, vmem, vmem),
+        out_specs=(hbm, vmem, vmem),
         scratch_shapes=[
             pltpu.VMEM((2 * NZ, tokens, OWN), bf16),
             pltpu.VMEM((tokens, width), bf16),
@@ -492,7 +459,6 @@
             pltpu.VMEM((own, width), f32),
             pltpu.VMEM((own, width), f32),
             pltpu.VMEM((NE, BLOCK, BLOCK), f32),
-            pltpu.VMEM((own, width), f32),
             pltpu.VMEM((own, width), f32),
             pltpu.VMEM((2, 4, 4, MSG, BLOCK), i16),
             pltpu.VMEM((2, 4, 4, MSG, BLOCK), i16),
@@ -515,7 +481,7 @@
             pltpu.VMEM((NE, BLOCK + 16, BLOCK), bf16),
             dma((2 * NZ,)),
             dma((4,)),
-            dma((4, 6)),
+            dma((4,)),
             dma((2, 4, 4)),
             dma((2, 4, 4)),
             dma((2, 4, 2)),
@@ -539,12 +505,13 @@
             collective_id=0, has_side_effects=True, vmem_limit_bytes=56 * 2**20
         ),
     )(acts, out_grads, master, moment_one, moment_two, routing, group_of)
+    weight, first, second = adam(master[0], moment_one[0], moment_two[0], grad)
     return (
-        weight,
-        first,
-        second,
+        weight[None],
+        first[None],
+        second[None],
         blocks.reshape(1, 1, NE, 1, BLOCK, BLOCK),
-        scales[:, 0, 0].reshape(1, 1, NE, 1),
+        scales[0, :NE].reshape(1, 1, NE, 1),
     )
 
 

time: 117 us -> 112 us (0.957)
  local copies, waits for them, and re-layouts: 7.97 us -> 2.06 us
  other arithmetic: 0 us -> 3.77 us
  Pallas kernels: 108 us -> 105 us
    unnamed x8 -> x9, local copies, waits for them, and re-layouts: 6.38 us -> 0.81 us
    broadcast_in_dim x0 -> x1, other arithmetic: none -> 3.77 us  [per_device(): second[None]]
    pallas_call x1, Pallas kernels: 108 us -> 105 us  [per_device(): pl.pallas_call(kernel, out_shape=(shape((own, width), f32), shape((NE, BL...]
    slice x1 -> x0, local copies, waits for them, and re-layouts: 1.59 us -> none  [per_device(): scales[:, 0, 0].reshape(1, 1, NE, 1)]
    another operation x0 -> x1, local copies, waits for them, and re-layouts: none -> 1.25 us  [per_device(): scales[0, :NE].reshape(1, 1, NE, 1)]
where the time goes in v2:
time: 112 us; the launch traced here: 111 us
  Pallas kernels  105 us (94%)
  other arithmetic  3.77 us (3%)
  local copies, waits for them, and re-layouts  2.06 us (2%)
    pallas_call x1, Pallas kernels, per_device(): pl.pallas_call(kernel, out_shape=(shape((own, width), f32), shape((NE, BL...  105 us
    broadcast_in_dim x1, other arithmetic, per_device(): second[None]  3.77 us

profile of v2, /device:TPU:1, one launch (start us, length us, event | category | flops | bytes accessed | tf_op | source)
XLA Modules:
  0.0 111.4 jit_solution(12685026341812656693)
XLA Ops:
  0.6 0.0 copy-start.2
  0.6 0.0 copy-start.1
  0.7 0.0 copy-start
  0.7 104.9 %update.1 = (f32[256,1024]{1,0:T(8,128)}, bf16[16,128,128]{2,1,0:T(8,128)(2,1)}, bf16[16,128]{1,0:T(8,128)(2,1)}) custom-call(bf16[1,512,4096]{2,1,0:T(8,128)(2,1)} %acts.1, bf16[1,512,1024]{2,1,0:T(8,128)(2,1)} %grads.1, f32[1,256,1024]{2,1,0:T(8,128)} %master.1, f32[1,256,1024]{2,1,0:T(8,128)} %moment_one.1, f32[1,256,1024]{2,1,0:T(8,128)} %moment_two.1, ...), custom_call_target="tpu_custom_call" | custom-call | flops 4294967296 | bytes 12582912 | tf_op jit(solution)/shard_map/update/pallas_call | solution.py:446
  105.6 0.0 copy-start.3
  105.6 1.3 %slice_bitcast_fusion = bf16[1,1,16,1]{2,3,1,0:T(2,128)(2,1)} fusion(bf16[16,128]{1,0:T(8,128)(2,1)} %get-tuple-element.10), kind=kLoop, calls=%fused_computation.10 | loop fusion | bytes 64 | tf_op jit(solution)/shard_map/reshape;squeeze | solution.py:514
  106.8 0.0 copy-done.2
  106.8 0.0 copy-done.1
  106.8 0.0 copy-done
  106.8 3.8 %fusion.5 = (f32[1,256,1024]{2,1,0:T(8,128)}, f32[1,256,1024]{2,1,0:T(8,128)}, f32[1,256,1024]{2,1,0:T(8,128)}) fusion(f32[256,1024]{1,0:T(8,128)} %get-tuple-element.8, f32[1,256,1024]{2,1,0:T(8,128)S(1)} %copy-done.2, f32[1,256,1024]{2,1,0:T(8,128)S(1)} %copy-done.1, f32[1,256,1024]{2,1,0:T(8,128)S(1)} %copy-done), kind=kLoop, calls=%fused_computation.9 | loop fusion | flops 3932160 | bytes 7340032 | tf_op jit(solution)/shard_map/broadcast_in_dim | solution.py:512
  110.6 0.0 copy-done.3
  110.6 0.8 copy.14
Async XLA Ops:
  0.6 106.2 %copy-start.2 = (f32[1,256,1024]{2,1,0:T(8,128)S(1)}, f32[1,256,1024]{2,1,0:T(8,128)}, u32[]{:S(2)}) copy-start(f32[1,256,1024]{2,1,0:T(8,128)} %moment_two.1) | copy-start | bytes 3145732
  0.6 106.2 %copy-start.1 = (f32[1,256,1024]{2,1,0:T(8,128)S(1)}, f32[1,256,1024]{2,1,0:T(8,128)}, u32[]{:S(2)}) copy-start(f32[1,256,1024]{2,1,0:T(8,128)} %moment_one.1) | copy-start | bytes 3145732
  0.7 106.2 %copy-start = (f32[1,256,1024]{2,1,0:T(8,128)S(1)}, f32[1,256,1024]{2,1,0:T(8,128)}, u32[]{:S(2)}) copy-start(f32[1,256,1024]{2,1,0:T(8,128)} %master.1) | copy-start | bytes 3145732
  105.6 5.0 %copy-start.3 = (bf16[16,128,128]{2,1,0:T(8,128)(2,1)S(1)}, bf16[16,128,128]{2,1,0:T(8,128)(2,1)}, u32[]{:S(2)}) copy-start(bf16[16,128,128]{2,1,0:T(8,128)(2,1)} %get-tuple-element.9) | copy-start | bytes 1572868

commit v3 on v2

--- a/solution.py
+++ b/solution.py
@@ -47,7 +47,9 @@
 def adam(weight, one, two, grad):
     first = beta_one * one + (1.0 - beta_one) * grad
     second = beta_two * two + (1.0 - beta_two) * grad * grad
-    update = first / corr_one / (jnp.sqrt(second / corr_two) + adam_eps) + decay_rate * weight
+    update = (first * (1.0 / corr_one)) / (
+        jnp.sqrt(second * (1.0 / corr_two)) + adam_eps
+    ) + decay_rate * weight
     return weight - learn_rate * update, first, second
 
 
@@ -77,9 +79,9 @@
     grad_out, blocks_out, scales_out,
     a_v, g_v, w_v, m_v, v_v, wt_v, sum_v,
     s1_send, s1_recv, s2_send, s2_recv, x2_send, x2_recv, x1_send, x1_recv, ask, asked, reply, replied,
-    stat_v, sel_v, place_v, answer_v, scale_v, r_send, r_recv,
+    stat_v, sel_v, place_v, answer_v, scale_v, r_send, r_recv, c_send, c_recv,
     a_sem, in_sem, out_sem,
-    s1_ss, s1_rs, s2_ss, s2_rs, x2_ss, x2_rs, x1_ss, x1_rs, ask_ss, ask_rs, rep_ss, rep_rs, r_ss, r_rs,
+    s1_ss, s1_rs, s2_ss, s2_rs, x2_ss, x2_rs, x1_ss, x1_rs, ask_ss, ask_rs, rep_ss, rep_rs, r_ss, r_rs, c_ss, c_rs,
 ):
     dp = lax.axis_index("dp")
     ex = lax.axis_index("expert")
@@ -311,6 +313,34 @@
         ask_copy(lax.rem(dp + k, ND), dp).start()
 
     asked[dp] = ask[...]
+
+    def roll_copy(slot, source):
+        return pltpu.make_async_remote_copy(
+            src_ref=r_send.at[slot], dst_ref=r_recv.at[source],
+            send_sem=r_ss.at[slot], recv_sem=r_rs.at[source],
+            device_id=(dp, slot), device_id_type=MESH,
+        )
+
+    def scale_copy(slot, source):
+        return pltpu.make_async_remote_copy(
+            src_ref=c_send.at[slot], dst_ref=c_recv.at[source],
+            send_sem=c_ss.at[slot], recv_sem=c_rs.at[source],
+            device_id=(dp, slot), device_id_type=MESH,
+        )
+
+    def held(slot):
+        b = jnp.int32(0)
+        for n in range(NE):
+            b = lax.select(routing[0, 0, n] == slot, jnp.int32(n), b)
+        return b
+
+    @pl.loop(1, NE)
+    def _(k):
+        slot = lax.rem(ex + k, NE)
+        r_send[slot] = wt_v[held(slot)]
+        roll_copy(slot, ex).start()
+
+    r_recv[ex] = wt_v[held(ex)]
     old = [along(x) for x in picked[1:]]
 
     @pl.loop(1, ND)
@@ -366,48 +396,37 @@
     for b in range(NE):
         scale_v[b] = jnp.broadcast_to(scale[b : b + 1, :], (8, BLOCK))
 
-    def roll_copy(slot, source):
-        return pltpu.make_async_remote_copy(
-            src_ref=r_send.at[slot], dst_ref=r_recv.at[source],
-            send_sem=r_ss.at[slot], recv_sem=r_rs.at[source],
-            device_id=(dp, slot), device_id_type=MESH,
-        )
-
-    def held(slot):
-        b = jnp.int32(0)
-        for n in range(NE):
-            b = lax.select(routing[0, 0, n] == slot, jnp.int32(n), b)
-        return b
-
-    def pack(ref, b):
-        wide = scale_v[b]
-        ref[:BLOCK, :] = (wt_v[b] / wide[0:1, :]).astype(jnp.bfloat16)
-        ref[BLOCK:, :] = jnp.broadcast_to(wide[0:1, :], (16, BLOCK)).astype(jnp.bfloat16)
-
     @pl.loop(1, NE)
     def _(k):
         slot = lax.rem(ex + k, NE)
-        pack(r_send.at[slot], held(slot))
-        roll_copy(slot, ex).start()
-
-    pack(r_recv.at[ex], held(ex))
+        c_send[slot] = scale_v[held(slot)]
+        scale_copy(slot, ex).start()
+
+    c_recv[ex] = scale_v[held(ex)]
 
     @pl.loop(1, NE)
     def _(k):
         source = lax.rem(ex + k, NE)
         roll_copy(source, source).wait_recv()
 
+    @pl.loop(1, NE)
+    def _(k):
+        source = lax.rem(ex + k, NE)
+        scale_copy(source, source).wait_recv()
+
     row = jnp.zeros((16, BLOCK), jnp.float32)
     for e in range(NE):
-        block = r_recv[group_of[e]]
-        blocks_out[e] = block[:BLOCK, :]
-        row = jnp.where(lanes == e, block[BLOCK:, :].astype(jnp.float32), row)
+        g = group_of[e]
+        wide = c_recv[g]
+        blocks_out[e] = (r_recv[g] / wide[0:1, :]).astype(jnp.bfloat16)
+        row = jnp.where(lanes == e, wide[0:1, :], row)
     scales_out[...] = row.astype(jnp.bfloat16)
 
     @pl.loop(1, NE)
     def _(k):
         slot = lax.rem(ex + k, NE)
         roll_copy(slot, ex).wait_send()
+        scale_copy(slot, ex).wait_send()
         peer = lax.rem(dp + k, ND)
         ask_copy(peer, dp).wait_send()
         reply_copy(peer, dp).wait_send()
@@ -477,8 +496,10 @@
             pltpu.VMEM((2, own, BLOCK), bf16),
             pltpu.VMEM((2, 8, BLOCK), f32),
             pltpu.VMEM((NE, 8, BLOCK), f32),
-            pltpu.VMEM((NE, BLOCK + 16, BLOCK), bf16),
-            pltpu.VMEM((NE, BLOCK + 16, BLOCK), bf16),
+            pltpu.VMEM((NE, BLOCK, BLOCK), f32),
+            pltpu.VMEM((NE, BLOCK, BLOCK), f32),
+            pltpu.VMEM((NE, 8, BLOCK), f32),
+            pltpu.VMEM((NE, 8, BLOCK), f32),
             dma((2 * NZ,)),
             dma((4,)),
             dma((4,)),
@@ -494,6 +515,8 @@
             dma((ND,)),
             dma((ND,)),
             dma((ND,)),
+            dma((NE,)),
+            dma((NE,)),
             dma((NE,)),
             dma((NE,)),
         ],

time: 112 us -> 110 us (0.982)
  Pallas kernels: 105 us -> 103 us
    pallas_call x1, Pallas kernels: 105 us -> 103 us  [per_device(): pl.pallas_call(kernel, out_shape=(shape((own, width), f32), shape((NE, BL...]
where the time goes in v3:
time: 110 us
  Pallas kernels  103 us (94%)
  other arithmetic  3.77 us (3%)
  local copies, waits for them, and re-layouts  2.06 us (2%)
    pallas_call x1, Pallas kernels, per_device(): pl.pallas_call(kernel, out_shape=(shape((own, width), f32), shape((NE, BL...  103 us
    broadcast_in_dim x1, other arithmetic, per_device(): second[None]  3.77 us

profile of v3, /device:TPU:1, one launch (start us, length us, event | category | flops | bytes accessed | tf_op | source)
XLA Modules:
  0.0 109.5 jit_solution(10123206857212660246)
XLA Ops:
  0.6 0.0 copy-start.2
  0.6 0.0 copy-start.1
  0.7 0.0 copy-start
  0.7 103.0 %update.1 = (f32[256,1024]{1,0:T(8,128)}, bf16[16,128,128]{2,1,0:T(8,128)(2,1)}, bf16[16,128]{1,0:T(8,128)(2,1)}) custom-call(bf16[1,512,4096]{2,1,0:T(8,128)(2,1)} %acts.1, bf16[1,512,1024]{2,1,0:T(8,128)(2,1)} %grads.1, f32[1,256,1024]{2,1,0:T(8,128)} %master.1, f32[1,256,1024]{2,1,0:T(8,128)} %moment_one.1, f32[1,256,1024]{2,1,0:T(8,128)} %moment_two.1, ...), custom_call_target="tpu_custom_call" | custom-call | flops 4294967296 | bytes 12582912 | tf_op jit(solution)/shard_map/update/pallas_call | solution.py:465
  103.7 0.0 copy-start.3
  103.7 1.3 %slice_bitcast_fusion = bf16[1,1,16,1]{2,3,1,0:T(2,128)(2,1)} fusion(bf16[16,128]{1,0:T(8,128)(2,1)} %get-tuple-element.10), kind=kLoop, calls=%fused_computation.10 | loop fusion | bytes 64 | tf_op jit(solution)/shard_map/reshape;squeeze | solution.py:537
  105.0 0.0 copy-done.2
  105.0 0.0 copy-done.1
  105.0 0.0 copy-done
  105.0 3.8 %fusion.5 = (f32[1,256,1024]{2,1,0:T(8,128)}, f32[1,256,1024]{2,1,0:T(8,128)}, f32[1,256,1024]{2,1,0:T(8,128)}) fusion(f32[256,1024]{1,0:T(8,128)} %get-tuple-element.8, f32[1,256,1024]{2,1,0:T(8,128)S(1)} %copy-done.2, f32[1,256,1024]{2,1,0:T(8,128)S(1)} %copy-done.1, f32[1,256,1024]{2,1,0:T(8,128)S(1)} %copy-done), kind=kLoop, calls=%fused_computation.9 | loop fusion | flops 3932160 | bytes 7340032 | tf_op jit(solution)/shard_map/broadcast_in_dim | solution.py:535
  108.7 0.0 copy-done.3
  108.7 0.8 copy.14
Async XLA Ops:
  0.6 104.3 %copy-start.2 = (f32[1,256,1024]{2,1,0:T(8,128)S(1)}, f32[1,256,1024]{2,1,0:T(8,128)}, u32[]{:S(2)}) copy-start(f32[1,256,1024]{2,1,0:T(8,128)} %moment_two.1) | copy-start | bytes 3145732
  0.6 104.3 %copy-start.1 = (f32[1,256,1024]{2,1,0:T(8,128)S(1)}, f32[1,256,1024]{2,1,0:T(8,128)}, u32[]{:S(2)}) copy-start(f32[1,256,1024]{2,1,0:T(8,128)} %moment_one.1) | copy-start | bytes 3145732
  0.7 104.3 %copy-start = (f32[1,256,1024]{2,1,0:T(8,128)S(1)}, f32[1,256,1024]{2,1,0:T(8,128)}, u32[]{:S(2)}) copy-start(f32[1,256,1024]{2,1,0:T(8,128)} %master.1) | copy-start | bytes 3145732
  103.7 5.0 %copy-start.3 = (bf16[16,128,128]{2,1,0:T(8,128)(2,1)S(1)}, bf16[16,128,128]{2,1,0:T(8,128)(2,1)}, u32[]{:S(2)}) copy-start(bf16[16,128,128]{2,1,0:T(8,128)(2,1)} %get-tuple-element.9) | copy-start | bytes 1572868

commit v4 on v3

--- a/solution.py
+++ b/solution.py
@@ -44,13 +44,18 @@
     return lax.select(k < half, pick(k, values[:half]), pick(k - half, values[half:]))
 
 
-def adam(weight, one, two, grad):
+def moments(one, two, grad):
     first = beta_one * one + (1.0 - beta_one) * grad
     second = beta_two * two + (1.0 - beta_two) * grad * grad
+    return first, second
+
+
+def adam(weight, one, two, grad):
+    first, second = moments(one, two, grad)
     update = (first * (1.0 / corr_one)) / (
         jnp.sqrt(second * (1.0 / corr_two)) + adam_eps
     ) + decay_rate * weight
-    return weight - learn_rate * update, first, second
+    return learn_rate * update
 
 
 def encode(ref, halves):
@@ -76,10 +81,10 @@
 
 def kernel(
     acts, grads, master, moment_one, moment_two, routing, group_of,
-    grad_out, blocks_out, scales_out,
-    a_v, g_v, w_v, m_v, v_v, wt_v, sum_v,
+    grad_out, step_out, blocks_out, scales_out,
+    a_v, g_v, w_v, m_v, v_v, wt_v, sum_v, step_v,
     s1_send, s1_recv, s2_send, s2_recv, x2_send, x2_recv, x1_send, x1_recv, ask, asked, reply, replied,
-    stat_v, sel_v, place_v, answer_v, scale_v, r_send, r_recv, c_send, c_recv,
+    stat_v, sel_v, place_v, scale_v, r_send, r_recv, c_send, c_recv,
     a_sem, in_sem, out_sem,
     s1_ss, s1_rs, s2_ss, s2_rs, x2_ss, x2_rs, x1_ss, x1_rs, ask_ss, ask_rs, rep_ss, rep_rs, r_ss, r_rs, c_ss, c_rs,
 ):
@@ -91,6 +96,10 @@
         return (lax.rem(z + 1 + 6 * way, NZ) * 2 + xh, ex)
 
     partner = (z * 2 + 1 - xh, ex)
+
+    def owner(dz, other):
+        return lax.rem(z + dz, NZ) * 2 + lax.rem(xh + other, 2)
+
     mine = z * 2 + xh
 
     def load_acts(off, half):
@@ -201,7 +210,10 @@
 
     def result(c):
         cols = pl.ds(pl.multiple_of(c * UC, UC), UC)
-        return pltpu.make_async_copy(sum_v.at[:, cols], grad_out.at[:, cols], out_sem.at[c])
+        return [
+            pltpu.make_async_copy(src.at[:, cols], dst.at[:, cols], out_sem.at[n, c])
+            for n, (src, dst) in enumerate(((sum_v, grad_out), (step_v, step_out)))
+        ]
 
     row_ids = lax.broadcasted_iota(jnp.int32, (BLOCK, BLOCK), 0)
 
@@ -209,7 +221,9 @@
         for h, grad in enumerate(halves):
             cols = pl.ds(pl.multiple_of(c * UC + h * BLOCK, BLOCK), BLOCK)
             sum_v[:, cols] = grad
-            weight = adam(w_v[:, cols], m_v[:, cols], v_v[:, cols], grad)[0]
+            step = adam(w_v[:, cols], m_v[:, cols], v_v[:, cols], grad)
+            step_v[:, cols] = step
+            weight = w_v[:, cols] - step
             for r in range(2):
                 b = r * 8 + 2 * c + h
                 rows = slice(r * BLOCK, (r + 1) * BLOCK)
@@ -225,7 +239,8 @@
                     stat_v[2 + n, pl.ds(b, 1), :] = jnp.sum(
                         jnp.where(one_row, src[rows, cols], 0.0), axis=0, keepdims=True
                     )
-        result(c).start()
+        for copy in result(c):
+            copy.start()
 
     def x1_task(c):
         encode(x1_send.at[c], s1_sum(1 - xh, c))
@@ -285,14 +300,14 @@
 
     def reply_copy(peer, source):
         return pltpu.make_async_remote_copy(
-            src_ref=reply.at[peer // 8], dst_ref=replied.at[source],
+            src_ref=reply.at[lax.rem(peer + dp, 2)], dst_ref=replied.at[source],
             send_sem=rep_ss.at[peer], recv_sem=rep_rs.at[source],
             device_id=(peer, ex), device_id_type=MESH,
         )
 
     lanes = lax.broadcasted_iota(jnp.int32, (NE, BLOCK), 1)
     blocks = lax.broadcasted_iota(jnp.int32, (NE, BLOCK), 0)
-    slots = lanes == lax.rem(dp, 8) * NE + blocks
+    slots = lanes % NE == blocks
     top = stat_v[0]
     most = jnp.max(top, axis=1, keepdims=True)
     lane = jnp.min(jnp.where(top == most, lanes, BLOCK), axis=1, keepdims=True)
@@ -308,9 +323,13 @@
         [jnp.broadcast_to(row_at, (8, BLOCK)), jnp.broadcast_to(col_at, (8, BLOCK))], axis=0
     )
 
-    @pl.loop(1, ND)
-    def _(k):
-        ask_copy(lax.rem(dp + k, ND), dp).start()
+    @pl.loop(0, NZ)
+    def _(dz):
+        ask_copy(owner(dz, 1), dp).start()
+
+    @pl.loop(1, NZ)
+    def _(dz):
+        ask_copy(owner(dz, 0), dp).start()
 
     asked[dp] = ask[...]
 
@@ -341,58 +360,66 @@
         roll_copy(slot, ex).start()
 
     r_recv[ex] = wt_v[held(ex)]
-    old = [along(x) for x in picked[1:]]
-
-    @pl.loop(1, ND)
-    def _(k):
-        source = lax.rem(dp + k, ND)
-        ask_copy(source, source).wait_recv()
-
-    for half in range(2):
-        total = asked[8 * half]
-        for n in range(1, 8):
-            total = total + asked[8 * half + n]
+    groups = lax.broadcasted_iota(jnp.int32, (16, BLOCK), 1) // NE
+    for other in range(2):
+
+        @pl.loop(1 - other, NZ)
+        def _(dz):
+            source = owner(dz, other)
+            ask_copy(source, source).wait_recv()
+
+        total = jnp.zeros((16, BLOCK), jnp.float32)
+        for dz in range(NZ):
+            total = jnp.where(groups == dz, asked[owner(dz, other)], total)
         rows = total[0:1, :].astype(jnp.int32)
         cols = total[8:9, :].astype(jnp.int32)
-        place_v[half] = (
-            lax.broadcasted_iota(jnp.int32, (OWN, BLOCK), 0) == rows
-        ).astype(jnp.float32).astype(jnp.bfloat16)
-        sel_v[half] = jnp.dot(
+        place_v[...] = (
+            (lax.broadcasted_iota(jnp.int32, (OWN, BLOCK), 0) == rows)
+            .astype(jnp.float32)
+            .astype(jnp.bfloat16)
+        )
+        sel_v[...] = jnp.dot(
             g_v[...],
             (lax.broadcasted_iota(jnp.int32, (g_v.shape[1], BLOCK), 0) == cols)
             .astype(jnp.float32)
             .astype(jnp.bfloat16),
             preferred_element_type=jnp.float32,
         )
-    answer_v[...] = jnp.zeros_like(answer_v)
-    groups = lax.broadcasted_iota(jnp.int32, (8, BLOCK), 1) // NE
-
-    @pl.loop(0, ND)
-    def _(o):
-        half = o // 8
-        chosen = jnp.dot(a_v[o], place_v[half], preferred_element_type=jnp.float32)
-        dots = jnp.sum(chosen * sel_v[half], axis=0, keepdims=True)
-        answer_v[half] = jnp.where(groups == lax.rem(o, 8), dots, answer_v[half])
-
-    reply[...] = answer_v[...]
-
-    @pl.loop(1, ND)
-    def _(k):
-        reply_copy(lax.rem(dp + k, ND), dp).start()
-
-    replied[dp] = answer_v[dp // 8]
+
+        def dots(quarter, answer, other=other):
+            for n in range(4):
+                dz = quarter * 4 + n
+                chosen = jnp.dot(
+                    a_v[owner(dz, other)], place_v[...], preferred_element_type=jnp.float32
+                )
+                answer = jnp.where(
+                    groups[:8] == dz, jnp.sum(chosen * sel_v[...], axis=0, keepdims=True), answer
+                )
+            return answer
+
+        reply[other] = lax.fori_loop(0, 2, dots, jnp.zeros((8, BLOCK), jnp.float32))
+
+        @pl.loop(1 - other, NZ)
+        def _(dz):
+            reply_copy(owner(dz, other), dp).start()
+
+    replied[dp] = reply[0]
 
     @pl.loop(1, ND)
     def _(k):
         source = lax.rem(dp + k, ND)
         reply_copy(source, source).wait_recv()
 
-    exact = replied[0]
-    for n in range(1, ND):
-        exact = exact + replied[n]
-    largest = jnp.abs(adam(*old, exact[0:1, :])[0])
+    exact = jnp.zeros((8, BLOCK), jnp.float32)
+    for other in range(2):
+        for dz in range(NZ):
+            exact = exact + jnp.where(
+                groups[:8] == (NZ - dz) % NZ, replied[owner(dz, other)], 0.0
+            )
+    exact = jnp.sum(jnp.where(slots, exact[0:1, :], 0.0), axis=1, keepdims=True)
+    old = [jnp.broadcast_to(x, (NE, BLOCK)) for x in picked[1:]]
+    largest = jnp.abs(old[0] - adam(*old, jnp.broadcast_to(exact, (NE, BLOCK))))
     scale = (largest + 1e-06).astype(jnp.bfloat16).astype(jnp.float32)
-    scale = jnp.sum(jnp.where(slots, scale, 0.0), axis=1, keepdims=True)
     for b in range(NE):
         scale_v[b] = jnp.broadcast_to(scale[b : b + 1, :], (8, BLOCK))
 
@@ -450,7 +477,8 @@
         x2_copy(j).wait_send()
 
     for c in range(4):
-        result(c).wait()
+        for copy in result(c):
+            copy.wait()
 
 
 def per_device(acts, out_grads, master, moment_one, moment_two, routing, group_of):
@@ -462,15 +490,16 @@
     smem = pl.BlockSpec(memory_space=pltpu.SMEM)
     vmem = pl.BlockSpec(memory_space=pltpu.VMEM)
     shape = jax.ShapeDtypeStruct
-    grad, blocks, scales = pl.pallas_call(
+    grad, step, blocks, scales = pl.pallas_call(
         kernel,
         out_shape=(
+            shape((own, width), f32),
             shape((own, width), f32),
             shape((NE, BLOCK, BLOCK), bf16),
             shape((16, BLOCK), bf16),
         ),
         in_specs=[hbm] * 5 + [smem] * 2,
-        out_specs=(hbm, vmem, vmem),
+        out_specs=(hbm, hbm, vmem, vmem),
         scratch_shapes=[
             pltpu.VMEM((2 * NZ, tokens, OWN), bf16),
             pltpu.VMEM((tokens, width), bf16),
@@ -478,6 +507,7 @@
             pltpu.VMEM((own, width), f32),
             pltpu.VMEM((own, width), f32),
             pltpu.VMEM((NE, BLOCK, BLOCK), f32),
+            pltpu.VMEM((own, width), f32),
             pltpu.VMEM((own, width), f32),
             pltpu.VMEM((2, 4, 4, MSG, BLOCK), i16),
             pltpu.VMEM((2, 4, 4, MSG, BLOCK), i16),
@@ -492,9 +522,8 @@
             pltpu.VMEM((2, 8, BLOCK), f32),
             pltpu.VMEM((ND, 8, BLOCK), f32),
             pltpu.VMEM((5, NE, BLOCK), f32),
-            pltpu.VMEM((2, tokens, BLOCK), f32),
-            pltpu.VMEM((2, own, BLOCK), bf16),
-            pltpu.VMEM((2, 8, BLOCK), f32),
+            pltpu.VMEM((tokens, BLOCK), f32),
+            pltpu.VMEM((own, BLOCK), bf16),
             pltpu.VMEM((NE, 8, BLOCK), f32),
             pltpu.VMEM((NE, BLOCK, BLOCK), f32),
             pltpu.VMEM((NE, BLOCK, BLOCK), f32),
@@ -502,7 +531,7 @@
             pltpu.VMEM((NE, 8, BLOCK), f32),
             dma((2 * NZ,)),
             dma((4,)),
-            dma((4,)),
+            dma((2, 4)),
             dma((2, 4, 4)),
             dma((2, 4, 4)),
             dma((2, 4, 2)),
@@ -528,7 +557,8 @@
             collective_id=0, has_side_effects=True, vmem_limit_bytes=56 * 2**20
         ),
     )(acts, out_grads, master, moment_one, moment_two, routing, group_of)
-    weight, first, second = adam(master[0], moment_one[0], moment_two[0], grad)
+    first, second = moments(moment_one[0], moment_two[0], grad)
+    weight = master[0] - step
     return (
         weight[None],
         first[None],

time: 110 us -> 106 us (0.964)
  Pallas kernels: 103 us -> 99.6 us
    pallas_call x1, Pallas kernels: 103 us -> 99.6 us  [per_device(): pl.pallas_call(kernel, out_shape=(shape((own, width), f32), shape((own, w...]
where the time goes in v4:
time: 106 us
  Pallas kernels  99.6 us (94%)
  other arithmetic  3.81 us (4%)
  local copies, waits for them, and re-layouts  2.01 us (2%)
    pallas_call x1, Pallas kernels, per_device(): pl.pallas_call(kernel, out_shape=(shape((own, width), f32), shape((own, w...  99.6 us
    broadcast_in_dim x1, other arithmetic, per_device(): second[None]  3.81 us

profile of v4, /device:TPU:1, one launch (start us, length us, event | category | flops | bytes accessed | tf_op | source)
XLA Modules:
  0.0 106.0 jit_solution(638806946310261867)
XLA Ops:
  0.6 0.0 copy-start.2
  0.6 0.0 copy-start.1
  0.7 0.0 copy-start
  0.7 99.6 %update.1 = (f32[256,1024]{1,0:T(8,128)}, f32[256,1024]{1,0:T(8,128)}, bf16[16,128,128]{2,1,0:T(8,128)(2,1)}, bf16[16,128]{1,0:T(8,128)(2,1)}) custom-call(bf16[1,512,4096]{2,1,0:T(8,128)(2,1)} %acts.1, bf16[1,512,1024]{2,1,0:T(8,128)(2,1)} %grads.1, f32[1,256,1024]{2,1,0:T(8,128)} %master.1, f32[1,256,1024]{2,1,0:T(8,128)} %moment_one.1, ...), custom_call_target="tpu_custom_call" | custom-call | flops 4294967296 | bytes 12582912 | tf_op jit(solution)/shard_map/update/pallas_call | solution.py:493
  100.2 1.2 %slice_bitcast_fusion = bf16[1,1,16,1]{2,3,1,0:T(2,128)(2,1)} fusion(bf16[16,128]{1,0:T(8,128)(2,1)} %get-tuple-element.12), kind=kLoop, calls=%fused_computation.7 | loop fusion | bytes 64 | tf_op jit(solution)/shard_map/reshape;squeeze | solution.py:567
  101.4 0.0 copy-done.2
  101.4 0.0 copy-done.1
  101.4 0.0 copy-done
  101.4 0.0 copy-start.3
  101.4 3.8 %fusion.1 = (f32[1,256,1024]{2,1,0:T(8,128)}, f32[1,256,1024]{2,1,0:T(8,128)}, f32[1,256,1024]{2,1,0:T(8,128)}) fusion(f32[256,1024]{1,0:T(8,128)} %get-tuple-element.10, f32[1,256,1024]{2,1,0:T(8,128)S(1)} %copy-done.2, f32[1,256,1024]{2,1,0:T(8,128)S(1)} %copy-done.1, f32[256,1024]{1,0:T(8,128)} %get-tuple-element.9, f32[1,256,1024]{2,1,0:T(8,128)S(1)} %copy-done), kind=kLoop, calls=%fused_computation.2 | loop fusion | flops 2097152 | bytes 8388608 | tf_op jit(solution)/shard_map/broadcast_in_dim | solution.py:565
  105.3 0.0 copy-done.3
  105.3 0.8 copy.14
Async XLA Ops:
  0.6 100.8 %copy-start.2 = (f32[1,256,1024]{2,1,0:T(8,128)S(1)}, f32[1,256,1024]{2,1,0:T(8,128)}, u32[]{:S(2)}) copy-start(f32[1,256,1024]{2,1,0:T(8,128)} %moment_two.1) | copy-start | bytes 3145732
  0.6 100.8 %copy-start.1 = (f32[1,256,1024]{2,1,0:T(8,128)S(1)}, f32[1,256,1024]{2,1,0:T(8,128)}, u32[]{:S(2)}) copy-start(f32[1,256,1024]{2,1,0:T(8,128)} %moment_one.1) | copy-start | bytes 3145732
  0.7 100.8 %copy-start = (f32[1,256,1024]{2,1,0:T(8,128)S(1)}, f32[1,256,1024]{2,1,0:T(8,128)}, u32[]{:S(2)}) copy-start(f32[1,256,1024]{2,1,0:T(8,128)} %master.1) | copy-start | bytes 3145732
  101.4 3.8 %copy-start.3 = (bf16[16,128,128]{2,1,0:T(8,128)(2,1)S(1)}, bf16[16,128,128]{2,1,0:T(8,128)(2,1)}, u32[]{:S(2)}) copy-start(bf16[16,128,128]{2,1,0:T(8,128)(2,1)} %get-tuple-element.11) | copy-start | bytes 1572868

commit v5 on v4

--- a/solution.py
+++ b/solution.py
@@ -112,6 +112,15 @@
     load_acts(4, 0).start()
     grads_copy.start()
     load_acts(4, 1).start()
+
+    barrier = pltpu.get_barrier_semaphore()
+    for peer in (zdev(0), zdev(1), partner):
+        pl.semaphore_signal(barrier, inc=1, device_id=peer, device_id_type=MESH)
+
+    @pl.loop(1, NE)
+    def _(k):
+        pl.semaphore_signal(barrier, inc=1, device_id=(dp, lax.rem(ex + k, NE)), device_id_type=MESH)
+
     order = (3, 5, 2, 6, 1, 7, 0)
     for off in order:
         for half in range(2):
@@ -123,14 +132,7 @@
     for c in state:
         c.start()
 
-    barrier = pltpu.get_barrier_semaphore()
-
-    @pl.loop(1, NE)
-    def _(k):
-        pl.semaphore_signal(barrier, inc=1, device_id=(lax.rem(dp + k, ND), ex), device_id_type=MESH)
-        pl.semaphore_signal(barrier, inc=1, device_id=(dp, lax.rem(ex + k, NE)), device_id_type=MESH)
-
-    pl.semaphore_wait(barrier, ND - 1 + NE - 1)
+    pl.semaphore_wait(barrier, 3 + NE - 1)
 
     def partial(i, c):
         p = lax.dot_general(

time: 106 us -> 106 us (level)
  no operation moved by 1% of the time
where the time goes in v5:
time: 106 us
  Pallas kernels  99.9 us (94%)
  other arithmetic  3.81 us (4%)
  local copies, waits for them, and re-layouts  2.01 us (2%)
    pallas_call x1, Pallas kernels, per_device(): pl.pallas_call(kernel, out_shape=(shape((own, width), f32), shape((own, w...  99.9 us
    broadcast_in_dim x1, other arithmetic, per_device(): second[None]  3.81 us

profile of v5, /device:TPU:1, one launch (start us, length us, event | category | flops | bytes accessed | tf_op | source)
XLA Modules:
  0.0 106.4 jit_solution(14380462920811365477)
XLA Ops:
  0.6 0.0 copy-start.2
  0.6 0.0 copy-start.1
  0.7 0.0 copy-start
  0.7 99.9 %update.1 = (f32[256,1024]{1,0:T(8,128)}, f32[256,1024]{1,0:T(8,128)}, bf16[16,128,128]{2,1,0:T(8,128)(2,1)}, bf16[16,128]{1,0:T(8,128)(2,1)}) custom-call(bf16[1,512,4096]{2,1,0:T(8,128)(2,1)} %acts.1, bf16[1,512,1024]{2,1,0:T(8,128)(2,1)} %grads.1, f32[1,256,1024]{2,1,0:T(8,128)} %master.1, f32[1,256,1024]{2,1,0:T(8,128)} %moment_one.1, ...), custom_call_target="tpu_custom_call" | custom-call | flops 4294967296 | bytes 12582912 | tf_op jit(solution)/shard_map/update/pallas_call | solution.py:495
  100.5 1.2 %slice_bitcast_fusion = bf16[1,1,16,1]{2,3,1,0:T(2,128)(2,1)} fusion(bf16[16,128]{1,0:T(8,128)(2,1)} %get-tuple-element.12), kind=kLoop, calls=%fused_computation.7 | loop fusion | bytes 64 | tf_op jit(solution)/shard_map/reshape;squeeze | solution.py:569
  101.7 0.0 copy-done.2
  101.7 0.0 copy-done.1
  101.7 0.0 copy-done
  101.7 0.0 copy-start.3
  101.7 3.8 %fusion.1 = (f32[1,256,1024]{2,1,0:T(8,128)}, f32[1,256,1024]{2,1,0:T(8,128)}, f32[1,256,1024]{2,1,0:T(8,128)}) fusion(f32[256,1024]{1,0:T(8,128)} %get-tuple-element.10, f32[1,256,1024]{2,1,0:T(8,128)S(1)} %copy-done.2, f32[1,256,1024]{2,1,0:T(8,128)S(1)} %copy-done.1, f32[256,1024]{1,0:T(8,128)} %get-tuple-element.9, f32[1,256,1024]{2,1,0:T(8,128)S(1)} %copy-done), kind=kLoop, calls=%fused_computation.2 | loop fusion | flops 2097152 | bytes 8388608 | tf_op jit(solution)/shard_map/broadcast_in_dim | solution.py:567
  105.6 0.0 copy-done.3
  105.6 0.8 copy.14
Async XLA Ops:
  0.6 101.1 %copy-start.2 = (f32[1,256,1024]{2,1,0:T(8,128)S(1)}, f32[1,256,1024]{2,1,0:T(8,128)}, u32[]{:S(2)}) copy-start(f32[1,256,1024]{2,1,0:T(8,128)} %moment_two.1) | copy-start | bytes 3145732
  0.6 101.1 %copy-start.1 = (f32[1,256,1024]{2,1,0:T(8,128)S(1)}, f32[1,256,1024]{2,1,0:T(8,128)}, u32[]{:S(2)}) copy-start(f32[1,256,1024]{2,1,0:T(8,128)} %moment_one.1) | copy-start | bytes 3145732
  0.7 101.1 %copy-start = (f32[1,256,1024]{2,1,0:T(8,128)S(1)}, f32[1,256,1024]{2,1,0:T(8,128)}, u32[]{:S(2)}) copy-start(f32[1,256,1024]{2,1,0:T(8,128)} %master.1) | copy-start | bytes 3145732
  101.7 3.8 %copy-start.3 = (bf16[16,128,128]{2,1,0:T(8,128)(2,1)S(1)}, bf16[16,128,128]{2,1,0:T(8,128)(2,1)}, u32[]{:S(2)}) copy-start(bf16[16,128,128]{2,1,0:T(8,128)(2,1)} %get-tuple-element.11) | copy-start | bytes 1572868

commit v6 on v4

--- a/solution.py
+++ b/solution.py
@@ -81,7 +81,7 @@
 
 def kernel(
     acts, grads, master, moment_one, moment_two, routing, group_of,
-    grad_out, step_out, blocks_out, scales_out,
+    grad_out, step_out, blocks_out, wide_out, scales_out,
     a_v, g_v, w_v, m_v, v_v, wt_v, sum_v, step_v,
     s1_send, s1_recv, s2_send, s2_recv, x2_send, x2_recv, x1_send, x1_recv, ask, asked, reply, replied,
     stat_v, sel_v, place_v, scale_v, r_send, r_recv, c_send, c_recv,
@@ -445,7 +445,8 @@
     for e in range(NE):
         g = group_of[e]
         wide = c_recv[g]
-        blocks_out[e] = (r_recv[g] / wide[0:1, :]).astype(jnp.bfloat16)
+        blocks_out[e] = r_recv[g]
+        wide_out[e] = wide
         row = jnp.where(lanes == e, wide[0:1, :], row)
     scales_out[...] = row.astype(jnp.bfloat16)
 
@@ -490,16 +491,17 @@
     smem = pl.BlockSpec(memory_space=pltpu.SMEM)
     vmem = pl.BlockSpec(memory_space=pltpu.VMEM)
     shape = jax.ShapeDtypeStruct
-    grad, step, blocks, scales = pl.pallas_call(
+    grad, step, blocks, wide, scales = pl.pallas_call(
         kernel,
         out_shape=(
             shape((own, width), f32),
             shape((own, width), f32),
-            shape((NE, BLOCK, BLOCK), bf16),
+            shape((NE, BLOCK, BLOCK), f32),
+            shape((NE, 8, BLOCK), f32),
             shape((16, BLOCK), bf16),
         ),
         in_specs=[hbm] * 5 + [smem] * 2,
-        out_specs=(hbm, hbm, vmem, vmem),
+        out_specs=(hbm, hbm, vmem, vmem, vmem),
         scratch_shapes=[
             pltpu.VMEM((2 * NZ, tokens, OWN), bf16),
             pltpu.VMEM((tokens, width), bf16),
@@ -557,6 +559,7 @@
             collective_id=0, has_side_effects=True, vmem_limit_bytes=56 * 2**20
         ),
     )(acts, out_grads, master, moment_one, moment_two, routing, group_of)
+    blocks = (blocks / wide[:, :1, :]).astype(bf16)
     first, second = moments(moment_one[0], moment_two[0], grad)
     weight = master[0] - step
     return (

time: 106 us -> 109 us (1.028)
  other arithmetic: 3.81 us -> 5.9 us
    unnamed x0 -> x1, other arithmetic: none -> 2.15 us
where the time goes in v6:
time: 109 us; the launch traced here: 108 us
  Pallas kernels  99.8 us (92%)
  other arithmetic  5.9 us (5%)
  local copies, waits for them, and re-layouts  2 us (2%)
    pallas_call x1, Pallas kernels, per_device(): pl.pallas_call(kernel, out_shape=(shape((own, width), f32), shape((own, w...  99.8 us
    broadcast_in_dim x1, other arithmetic, per_device(): second[None]  3.76 us

profile of v6, /device:TPU:1, one launch (start us, length us, event | category | flops | bytes accessed | tf_op | source)
XLA Modules:
  0.0 108.4 jit_solution(16764620308370118687)
XLA Ops:
  0.6 0.0 copy-start.2
  0.6 0.0 copy-start.1
  0.7 0.0 copy-start
  0.7 99.8 %update.1 = (f32[256,1024]{1,0:T(8,128)}, f32[256,1024]{1,0:T(8,128)}, f32[16,128,128]{2,1,0:T(8,128)}, f32[16,8,128]{2,1,0:T(8,128)}, bf16[16,128]{1,0:T(8,128)(2,1)}) custom-call(bf16[1,512,4096]{2,1,0:T(8,128)(2,1)} %acts.1, bf16[1,512,1024]{2,1,0:T(8,128)(2,1)} %grads.1, f32[1,256,1024]{2,1,0:T(8,128)} %master.1, f32[1,256,1024]{2,1,0:T(8,128)} %moment_one.1, ...), custom_call_target="tpu_custom_call" | custom-call | flops 4294967296 | bytes 12582912 | tf_op jit(solution)/shard_map/update/pallas_call | solution.py:494
  100.4 1.1 %slice_bitcast_fusion = bf16[1,1,16,1]{2,3,1,0:T(2,128)(2,1)} fusion(bf16[16,128]{1,0:T(8,128)(2,1)} %get-tuple-element.14), kind=kLoop, calls=%fused_computation.9 | loop fusion | bytes 64 | tf_op jit(solution)/shard_map/reshape;squeeze | solution.py:570
  101.6 0.8 slice.6
  102.4 2.1 %fusion.4 = bf16[1,1,16,1,128,128]{5,4,3,2,1,0:T(8,128)(2,1)} fusion(f32[16,128,128]{2,1,0:T(8,128)} %get-tuple-element.12, f32[16,128]{1,0:T(8,128)S(1)} %bitcast.23), kind=kLoop, calls=%fused_computation.8 | loop fusion | flops 524288 | bytes 1581056
  104.6 0.0 copy-done.2
  104.6 0.0 copy-done.1
  104.6 0.0 copy-done
  104.6 3.8 %fusion.1 = (f32[1,256,1024]{2,1,0:T(8,128)}, f32[1,256,1024]{2,1,0:T(8,128)}, f32[1,256,1024]{2,1,0:T(8,128)}) fusion(f32[256,1024]{1,0:T(8,128)} %get-tuple-element.11, f32[1,256,1024]{2,1,0:T(8,128)S(1)} %copy-done.2, f32[1,256,1024]{2,1,0:T(8,128)S(1)} %copy-done.1, f32[256,1024]{1,0:T(8,128)} %get-tuple-element.10, f32[1,256,1024]{2,1,0:T(8,128)S(1)} %copy-done), kind=kLoop, calls=%fused_computation.2 | loop fusion | flops 2097152 | bytes 8388608 | tf_op jit(solution)/shard_map/broadcast_in_dim | solution.py:568
Async XLA Ops:
  0.6 104.0 %copy-start.2 = (f32[1,256,1024]{2,1,0:T(8,128)S(1)}, f32[1,256,1024]{2,1,0:T(8,128)}, u32[]{:S(2)}) copy-start(f32[1,256,1024]{2,1,0:T(8,128)} %moment_two.1) | copy-start | bytes 3145732
  0.6 103.9 %copy-start.1 = (f32[1,256,1024]{2,1,0:T(8,128)S(1)}, f32[1,256,1024]{2,1,0:T(8,128)}, u32[]{:S(2)}) copy-start(f32[1,256,1024]{2,1,0:T(8,128)} %moment_one.1) | copy-start | bytes 3145732
  0.7 103.9 %copy-start = (f32[1,256,1024]{2,1,0:T(8,128)S(1)}, f32[1,256,1024]{2,1,0:T(8,128)}, u32[]{:S(2)}) copy-start(f32[1,256,1024]{2,1,0:T(8,128)} %master.1) | copy-start | bytes 3145732
